TPU v7x, 32 devices: a whole 2x2x4 slice. The times are simulated.
32 devices in a mesh: stream: 4 (over z), span: 8 (over y, x, core).
Axes of the slice: x: 2, y: 2, z: 4, core: 2. Of those that a mesh axis runs over, the one named last changes fastest.
Arguments:
- velocity: float32 [3, 32, 128, 1024], P(None, 'stream', 'span'), may hold values from -36 to 36
- coefficient: float32 [32, 128, 1024], P('stream', 'span'), may hold values from 0.5 to 4
- coords: float32 [3, 4096], P(None, ('stream', 'span')), may hold values from -1 to 1
- forces: float32 [3, 4096], P(None, ('stream', 'span')), may hold values from -12 to 12
- line_id: int32 [4096], P(('stream', 'span')), may hold values from 0 to 399
- line_gain: float32 [400], replicated, may hold values from 0.5 to 2
- dest_span: int32 [4096, 1], P(('stream', 'span')), may hold values from 0 to 7; in each aligned block of 128 rows (0 to 127, 128 to 255, ...) at most 32 rows name the same one
- owner_element: int32 [4096], P(('stream', 'span')), may hold values from 0 to 255
Outputs:
- pressure: float32 [32, 128, 1024], P('stream', 'span')
- residual: float32 [32, 128, 1024], P('stream', 'span')
Inputs may be any that keep to these rules, and one draw needn't show every extreme that they name: `dest_span`: of the 128 blade points of one device, at most 32 name the same span index, and in every draw some span index is named by exactly 32 of one device's points. `owner_element`: an element of the device at the point's span index in the same slab, numbered (ex * 2 + ey) * 128 + ez.
All inputs are finite; a program needn't handle non-finite values.
Results may differ from a plain program's by a relative error of at most 0.00019.
Values sent between devices are 32-bit elements; how exact they have to be, the bound alone decides.
A program may use at most 64 MiB of HBM per device.

v0:
```python
import functools

import jax
import jax.numpy as jnp
import numpy as np
from jax import lax
from jax.experimental import pallas as pl
from jax.experimental.pallas import tpu as pltpu
from jax.sharding import PartitionSpec as P

POLY = 8
ITERS = 3
LANES = 128
CHUNK = 256

kernel_width = 0.45
gll_nodes = [
    -1.0,
    -0.8717401485096066,
    -0.5917001814331423,
    -0.2092992179024789,
    0.2092992179024789,
    0.5917001814331423,
    0.8717401485096066,
    1.0,
]
MESH = pl.DeviceIdType.MESH
PAIRS = [(0, 0), (0, 1), (1, 1), (0, 2), (1, 2), (2, 2), (0, 3), (1, 3), (2, 3)]
OFFSETS = [(1, 0), (-1, 0), (0, 1), (0, -1), (1, 1), (1, -1), (-1, 1), (-1, -1)]


def legendre_value(point, degree):
    previous = 1.0
    current = point
    for order in range(1, degree):
        following = ((2 * order + 1) * point * current - order * previous) / (order + 1)
        previous = current
        current = following
    return current


def gll_tables():
    degree = POLY - 1
    values = [legendre_value(point, degree) for point in gll_nodes]
    weights = [2.0 / (degree * (degree + 1) * value * value) for value in values]
    diffmat = np.zeros((POLY, POLY))
    for i in range(POLY):
        for j in range(POLY):
            if i != j:
                diffmat[i, j] = values[i] / (values[j] * (gll_nodes[i] - gll_nodes[j]))
    diffmat[0, 0] = -degree * (degree + 1) / 4.0
    diffmat[-1, -1] = degree * (degree + 1) / 4.0
    return (
        np.asarray(gll_nodes, np.float32),
        np.asarray(weights, np.float32),
        np.asarray(diffmat, np.float32),
    )


def split_np(matrix):
    high = matrix.astype(jnp.bfloat16)
    low = (matrix - high.astype(np.float32)).astype(jnp.bfloat16)
    return high, low


def constants(extent0, extent1):
    nodes, weights, diffmat = gll_tables()
    eye = functools.partial(np.eye, dtype=np.float32)
    along0 = np.kron(eye(extent0 // POLY), np.kron(diffmat, eye(extent1)))
    along1 = np.kron(eye(extent0 * extent1 // POLY), diffmat)
    rows = np.concatenate([along0, along1], axis=0)
    cols = np.kron(eye(CHUNK // POLY), diffmat)

    def left(matrix):
        high, low = split_np(matrix)
        return np.concatenate([high, high, low], axis=1)

    def right(matrix):
        high, low = split_np(matrix)
        return np.concatenate([high, high, low], axis=0)

    row_weight = np.kron(np.tile(weights, extent0 // POLY), np.tile(weights, extent1 // POLY))
    row_weight = row_weight.astype(np.float32)
    weight = row_weight[:, None] * np.tile(weights, CHUNK // POLY)[None, :]
    column = np.repeat(nodes[:, None], LANES, axis=1)
    return left(rows), left(rows.T.copy()), right(cols.T.copy()), right(cols), weight, column


def split2(value):
    high = value.astype(jnp.bfloat16)
    low = (value - high.astype(jnp.float32)).astype(jnp.bfloat16)
    return high, low


def split3(value):
    high = value.astype(jnp.bfloat16)
    rest = value - high.astype(jnp.float32)
    middle = rest.astype(jnp.bfloat16)
    low = (rest - middle.astype(jnp.float32)).astype(jnp.bfloat16)
    return high, middle, low


def dot(first, second):
    return jnp.dot(first, second, preferred_element_type=jnp.float32)


def dot_nt(first, second):
    return lax.dot_general(
        first, second, (((1,), (1,)), ((), ())), preferred_element_type=jnp.float32
    )


def stacked(value, axis):
    high, low = split2(value)
    return jnp.concatenate([high, low, high], axis=axis)


def combine(first, second, gram):
    total = 0.0
    for i, x in enumerate(first):
        for j, y in enumerate(second):
            if x is not None and y is not None:
                total = total + x * y * gram[(min(i, j), max(i, j))]
    return total


def body(
    sizes,
    velocity,
    coefficient,
    coords,
    forces,
    line_id,
    line_gain,
    dest_span,
    owner,
    rows_fwd,
    rows_bwd,
    cols_fwd,
    cols_bwd,
    weight,
    nodes,
    pressure,
    residual,
    vel,
    metric,
    basis,
    work,
    inv_mult,
    out_pts,
    in_pts,
    lhs_pts,
    rhs_pts,
    send_stream,
    recv_stream,
    send_span,
    recv_span,
    send_edge,
    recv_edge,
    sums1,
    sums2,
    load_sem,
    pts_send,
    pts_recv,
    halo_send,
    halo_recv,
    sum1_send,
    sum1_recv,
    sum2_send,
    sum2_recv,
):
    n_stream, n_span, extent0, extent1, extent2, capacity = sizes
    rows = extent0 * extent1
    me_s, me_p = lax.axis_index("stream"), lax.axis_index("span")

    loads = [pltpu.make_async_copy(velocity.at[c], vel.at[c], load_sem.at[c]) for c in range(3)]
    loads.append(pltpu.make_async_copy(coefficient, metric, load_sem.at[3]))
    for load in loads:
        load.start()

    def exists(offset):
        s, p = me_s + offset[0], me_p + offset[1]
        return (s >= 0) & (s < n_stream) & (p >= 0) & (p < n_span)

    def at_offset(offset):
        return (
            lax.rem(me_s + offset[0] + n_stream, n_stream),
            lax.rem(me_p + offset[1] + n_span, n_span),
        )

    span_peers = [lax.rem(me_p + j, n_span) for j in range(1, n_span)]
    stream_peers = [lax.rem(me_s + j, n_stream) for j in range(1, n_stream)]

    barrier = pltpu.get_barrier_semaphore()
    for peer in span_peers:
        pl.semaphore_signal(barrier, inc=1, device_id=(me_s, peer), device_id_type=MESH)
    for peer in stream_peers:
        pl.semaphore_signal(barrier, inc=1, device_id=(peer, me_p), device_id_type=MESH)
    greeted = n_span - 1 + n_stream - 1
    for offset in OFFSETS[4:]:

        @pl.when(exists(offset))
        def _(offset=offset):
            pl.semaphore_signal(
                barrier, inc=1, device_id=at_offset(offset), device_id_type=MESH
            )

        greeted = greeted + exists(offset).astype(jnp.int32)

    points = coords.shape[1]
    group = LANES // capacity
    groups = n_span // group
    lines = line_gain.shape[1]
    ids = line_id[...]
    chosen = (lax.broadcasted_iota(jnp.int32, (lines, points), 0) == ids).astype(jnp.bfloat16)
    gain = sum(dot(part, chosen) for part in reversed(split3(line_gain[...])))
    scaled = forces[...] * gain
    target = dest_span[...]
    spans_at = lax.broadcasted_iota(jnp.int32, (n_span, points), 0)
    named = (spans_at == target).astype(jnp.float32)
    earlier = (
        lax.broadcasted_iota(jnp.int32, (points, points), 0)
        < lax.broadcasted_iota(jnp.int32, (points, points), 1)
    ).astype(jnp.bfloat16)
    before = dot(named.astype(jnp.bfloat16), earlier)
    rank = jnp.sum(named * before, axis=0, keepdims=True).astype(jnp.int32)
    slot = target * LANES + lax.rem(me_p, group) * capacity + rank
    payload = jnp.concatenate(
        [
            coords[...],
            scaled,
            owner[...].astype(jnp.float32),
            jnp.zeros((1, points), jnp.float32),
        ],
        axis=0,
    )
    parts = jnp.concatenate(
        [p.astype(jnp.float32) for p in split3(payload)], axis=0
    ).astype(jnp.bfloat16)
    for dest in range(n_span):
        placed = (
            lax.broadcasted_iota(jnp.int32, (LANES, points), 0) + dest * LANES == slot
        ).astype(jnp.float32).astype(jnp.bfloat16)
        tile = dot_nt(parts, placed)
        out_pts[dest] = (tile[16:24] + tile[8:16]) + tile[0:8]

    pl.semaphore_wait(barrier, greeted)

    def points_copy(peer, slot_at):
        return pltpu.make_async_remote_copy(
            src_ref=out_pts.at[peer],
            dst_ref=in_pts.at[slot_at],
            send_sem=pts_send.at[peer],
            recv_sem=pts_recv.at[slot_at],
            device_id=(me_s, peer),
            device_id_type=MESH,
        )

    for peer in span_peers:
        points_copy(peer, me_p).start()
    in_pts[me_p] = out_pts[me_p]

    row_at = lax.broadcasted_iota(jnp.int32, (rows, LANES), 0)
    lane_at = lax.broadcasted_iota(jnp.int32, (rows, LANES), 1)
    at0, at1 = row_at // extent1, row_at % extent1
    pos0 = me_s * extent0 + at0
    pos1 = me_p * extent1 + at1

    def halves(node, inner):
        face = (node == 0) | (node == POLY - 1)
        return jnp.where(face & inner, 0.5, 1.0).astype(jnp.float32)

    mult = halves(at0 % POLY, (pos0 > 0) & (pos0 < extent0 * n_stream - 1))
    mult = mult * halves(at1 % POLY, (pos1 > 0) & (pos1 < extent1 * n_span - 1))
    for block in range(extent2 // LANES):
        pos2 = block * LANES + lane_at
        here = mult * halves(pos2 % POLY, (pos2 > 0) & (pos2 < extent2 - 1))
        inv_mult[:, block * LANES : (block + 1) * LANES] = here

    chunks = [slice(c, c + CHUNK) for c in range(0, extent2, CHUNK)]
    loads[3].wait()
    for cols in chunks:
        metric[:, cols] = metric[:, cols] * weight[...]

    for peer in span_peers:
        points_copy(peer, peer).wait_recv()

    elems2 = extent2 // POLY
    total_pts = groups * LANES
    arrived = []
    for g in range(groups):
        tile = in_pts[g * group]
        for i in range(1, group):
            tile = tile + in_pts[g * group + i]
        arrived.append(tile)
    node_col = nodes[...]
    for g in range(groups):
        tile = arrived[g]
        lanes = slice(g * LANES, (g + 1) * LANES)
        kern = [
            jnp.exp(-(((node_col - tile[k : k + 1]) / kernel_width) ** 2)) for k in range(3)
        ]
        elem = tile[6:7].astype(jnp.int32)
        elem_y = lax.rem(lax.div(elem, elems2), extent1 // POLY)
        elem_x = lax.div(elem, elems2 * (extent1 // POLY))
        elem_z = lax.rem(elem, elems2)
        for c in range(3):
            for a in range(extent0):
                for ey in range(extent1 // POLY):
                    mine = (elem_x == a // POLY) & (elem_y == ey)
                    factor = jnp.where(mine, tile[3 + c : 4 + c] * kern[0][a % POLY : a % POLY + 1], 0.0)
                    base = c * rows + a * extent1 + ey * POLY
                    lhs_pts[base : base + POLY, lanes] = factor * kern[1]
        for ez in range(elems2):
            rhs_pts[ez * POLY : (ez + 1) * POLY, lanes] = jnp.where(elem_z == ez, kern[2], 0.0)

    left_pts = stacked(lhs_pts[...], 1)

    def rhs_chunk(cols):
        high, low = split2(rhs_pts[cols, :])
        force = dot_nt(left_pts, jnp.concatenate([high, high, low], axis=1))
        part = [weight[...] * (vel[c, :, cols] + force[c * rows : (c + 1) * rows]) for c in range(3)]
        both = jnp.concatenate(part[:2], axis=0)
        work[:, cols] = dot(rows_bwd[...], stacked(both, 0)) + dot(
            stacked(part[2], 1), cols_bwd[...]
        )

    def operator_chunk(k, cols):
        field = basis[k, :, cols]
        high, low = split2(field)
        m = metric[:, cols]
        grad = dot(rows_fwd[...], jnp.concatenate([high, low, high], axis=0))
        grad2 = dot(jnp.concatenate([high, low, high], axis=1), cols_fwd[...])
        both = jnp.concatenate([grad[:rows] * m, grad[rows:] * m], axis=0)
        work[:, cols] = (
            dot(rows_bwd[...], stacked(both, 0))
            + dot(stacked(grad2 * m, 1), cols_bwd[...])
            + weight[...] * field
        )

    last0, last1 = extent0 - 1, extent1 - 1

    def halo_copy(k, d):
        offset = OFFSETS[d]
        if d < 2:
            src, dst = send_stream.at[k, d], recv_stream.at[k, d]
        elif d < 4:
            src, dst = send_span.at[k, d - 2], recv_span.at[k, d - 2]
        else:
            src, dst = send_edge.at[k, d - 4], recv_edge.at[k, d - 4]
        return pltpu.make_async_remote_copy(
            src_ref=src,
            dst_ref=dst,
            send_sem=halo_send.at[k, d],
            recv_sem=halo_recv.at[k, d],
            device_id=at_offset(offset),
            device_id_type=MESH,
        )

    def halo_start(k, d):
        @pl.when(exists(OFFSETS[d]))
        def _():
            halo_copy(k, d).start()

    def from_offset(d):
        return exists((-OFFSETS[d][0], -OFFSETS[d][1]))

    def assemble(k):
        lane = lax.broadcasted_iota(jnp.int32, (POLY, extent2), 1)
        first2 = (lane % POLY == 0) & (lane > 0)
        last2 = (lane % POLY == POLY - 1) & (lane < extent2 - 1)
        sub = lax.broadcasted_iota(jnp.int32, (POLY, extent2), 0)
        order = [0, last0] + list(range(1, last0))
        for a in order:
            tiles = []
            for ey in range(extent1 // POLY):
                base = a * extent1 + ey * POLY
                x = work[base : base + POLY, :]
                lower = pltpu.roll(x, 1, 1)
                upper = pltpu.roll(x, extent2 - 1, 1)
                tiles.append(x + jnp.where(first2, lower, 0.0) + jnp.where(last2, upper, 0.0))
            joined = []
            for ey, x in enumerate(tiles):
                y = x
                if ey > 0:
                    y = y + jnp.where(sub == 0, pltpu.roll(tiles[ey - 1], 1, 0), 0.0)
                if ey + 1 < len(tiles):
                    y = y + jnp.where(
                        sub == POLY - 1, pltpu.roll(tiles[ey + 1], POLY - 1, 0), 0.0
                    )
                joined.append(y)
            for ey, y in enumerate(joined):
                base = a * extent1 + ey * POLY
                basis[k, base : base + POLY, :] = y
                if a == last0:
                    send_stream[k, 0, ey * POLY : (ey + 1) * POLY, :] = y
                if a == 0:
                    send_stream[k, 1, ey * POLY : (ey + 1) * POLY, :] = y
            top, bottom = joined[-1][POLY - 1 : POLY], joined[0][0:1]
            send_span[k, 0, a : a + 1, :] = top
            send_span[k, 1, a : a + 1, :] = bottom
            if a == last0:
                send_edge[k, 0] = top
                send_edge[k, 1] = bottom
                for d in (0, 4, 5):
                    halo_start(k, d)
            if a == 0:
                send_edge[k, 2] = top
                send_edge[k, 3] = bottom
                for d in (1, 6, 7):
                    halo_start(k, d)
        halo_start(k, 2)
        halo_start(k, 3)

        def arrive(d, base, count):
            @pl.when(from_offset(d))
            def _():
                halo_copy(k, d).wait_recv()
                basis[k, base : base + count, :] = (
                    basis[k, base : base + count, :] + recv_stream[k, d]
                )

        def arrive_span(d, at):
            @pl.when(from_offset(d))
            def _():
                halo_copy(k, d).wait_recv()
                for a in range(extent0):
                    row = a * extent1 + at
                    basis[k, row : row + 1, :] = (
                        basis[k, row : row + 1, :] + recv_span[k, d - 2, a : a + 1, :]
                    )

        def arrive_edge(d, row):
            @pl.when(from_offset(d))
            def _():
                halo_copy(k, d).wait_recv()
                basis[k, row : row + 1, :] = basis[k, row : row + 1, :] + recv_edge[k, d - 4]

        arrive_span(2, 0)
        arrive_span(3, last1)
        arrive_edge(4, 0)
        arrive_edge(5, last1)
        arrive_edge(6, last0 * extent1)
        arrive_edge(7, last0 * extent1 + last1)
        arrive(0, 0, extent1)
        arrive(1, last0 * extent1, extent1)

    for load in loads[:3]:
        load.wait()
    for cols in chunks:
        rhs_chunk(cols)
    assemble(0)
    for k in range(ITERS):
        for cols in chunks:
            operator_chunk(k, cols)
        assemble(k + 1)

    def partial(step, totals):
        at = pl.ds(pl.multiple_of(step * POLY, POLY), POLY)
        mult_at = inv_mult[at, :]
        vec = [basis[i, at, :] for i in range(ITERS + 1)]
        scaled_vec = [vec[i] * mult_at for i in range(ITERS)]
        new = []
        for total, (i, j) in zip(totals, PAIRS):
            prod = scaled_vec[i] * vec[j]
            for block in range(extent2 // LANES):
                total = total + prod[:, block * LANES : (block + 1) * LANES]
            new.append(total)
        return tuple(new)

    totals = lax.fori_loop(
        0,
        rows // POLY,
        partial,
        tuple(jnp.zeros((POLY, LANES), jnp.float32) for _ in PAIRS),
    )
    mine = [jnp.sum(total, axis=0, keepdims=True) for total in totals]
    mine.append(jnp.zeros((16 - len(PAIRS), LANES), jnp.float32))
    sums1[me_p] = jnp.concatenate(mine, axis=0)

    def sum1_copy(peer, slot_at):
        return pltpu.make_async_remote_copy(
            src_ref=sums1.at[me_p],
            dst_ref=sums1.at[slot_at],
            send_sem=sum1_send.at[peer],
            recv_sem=sum1_recv.at[slot_at],
            device_id=(me_s, peer),
            device_id_type=MESH,
        )

    def sum2_copy(peer, slot_at):
        return pltpu.make_async_remote_copy(
            src_ref=sums2.at[me_s],
            dst_ref=sums2.at[slot_at],
            send_sem=sum2_send.at[peer],
            recv_sem=sum2_recv.at[slot_at],
            device_id=(peer, me_p),
            device_id_type=MESH,
        )

    for peer in span_peers:
        sum1_copy(peer, me_p).start()
    for peer in span_peers:
        sum1_copy(peer, peer).wait_recv()
    total = sums1[0]
    for i in range(1, n_span):
        total = total + sums1[i]
    sums2[me_s] = total
    for peer in stream_peers:
        sum2_copy(peer, me_s).start()
    for peer in stream_peers:
        sum2_copy(peer, peer).wait_recv()
    total = sums2[0]
    for i in range(1, n_stream):
        total = total + sums2[i]
    total = jnp.broadcast_to(jnp.sum(total, axis=1, keepdims=True), (16, LANES))
    gram = {pair: total[n : n + 1] for n, pair in enumerate(PAIRS)}

    one = jnp.ones((1, LANES), jnp.float32)
    res, direction, pres = [one], [one], [None] * ITERS
    norm = gram[(0, 0)]
    for iteration in range(ITERS):
        applied = [None] + direction
        step_len = norm / combine(direction, applied, gram)
        for i, x in enumerate(direction):
            pres[i] = step_len * x if pres[i] is None else pres[i] + step_len * x
        new_res = []
        for i, x in enumerate(applied):
            old = res[i] if i < len(res) else None
            if x is None:
                new_res.append(old)
            elif old is None:
                new_res.append(-(step_len * x))
            else:
                new_res.append(old - step_len * x)
        res = new_res
        if iteration + 1 < ITERS:
            norm_next = combine(res, res, gram)
            ratio = norm_next / norm
            direction = [
                x + ratio * direction[i] if i < len(direction) else x for i, x in enumerate(res)
            ]
            norm = norm_next

    pres = [jnp.broadcast_to(x[:, 0:1], (POLY, extent2)) for x in pres]
    res = [jnp.broadcast_to(x[:, 0:1], (POLY, extent2)) for x in res]

    def finish(step, carry):
        at = pl.ds(pl.multiple_of(step * POLY, POLY), POLY)
        vec = [basis[i, at, :] for i in range(ITERS + 1)]
        out = pres[0] * vec[0]
        for i in range(1, ITERS):
            out = out + pres[i] * vec[i]
        pressure[at, :] = out
        out = res[0] * vec[0]
        for i in range(1, ITERS + 1):
            out = out + res[i] * vec[i]
        residual[at, :] = out
        return carry

    lax.fori_loop(0, rows // POLY, finish, 0)

    for peer in span_peers:
        points_copy(peer, me_p).wait_send()
        sum1_copy(peer, me_p).wait_send()
    for peer in stream_peers:
        sum2_copy(peer, me_s).wait_send()
    for k in range(ITERS + 1):
        for d in range(len(OFFSETS)):

            @pl.when(exists(OFFSETS[d]))
            def _(k=k, d=d):
                halo_copy(k, d).wait_send()


def on_device(velocity, coefficient, coords, forces, line_id, line_gain, dest_span, owner_element):
    extent0, extent1, extent2 = coefficient.shape
    rows = extent0 * extent1
    points = coords.shape[1]
    n_stream, n_span = lax.axis_size("stream"), lax.axis_size("span")
    capacity = max(2, 2 * points // n_span)
    total_pts = n_span * capacity
    tables = constants(extent0, extent1)
    f32 = jnp.float32
    block = jax.ShapeDtypeStruct((rows, extent2), f32)
    vmem = pl.BlockSpec(memory_space=pltpu.VMEM)
    hbm = pl.BlockSpec(memory_space=pl.ANY)
    steps = ITERS + 1
    sizes = (n_stream, n_span, extent0, extent1, extent2, capacity)
    pressure, residual = pl.pallas_call(
        functools.partial(body, sizes),
        out_shape=(block, block),
        in_specs=[hbm, hbm] + [vmem] * 12,
        out_specs=(vmem, vmem),
        scratch_shapes=[
            pltpu.VMEM((3, rows, extent2), f32),
            pltpu.VMEM((rows, extent2), f32),
            pltpu.VMEM((steps, rows, extent2), f32),
            pltpu.VMEM((rows, extent2), f32),
            pltpu.VMEM((rows, extent2), f32),
            pltpu.VMEM((n_span, 8, LANES), f32),
            pltpu.VMEM((n_span, 8, LANES), f32),
            pltpu.VMEM((3 * rows, total_pts), f32),
            pltpu.VMEM((extent2, total_pts), f32),
            pltpu.VMEM((steps, 2, extent1, extent2), f32),
            pltpu.VMEM((steps, 2, extent1, extent2), f32),
            pltpu.VMEM((steps, 2, extent0, extent2), f32),
            pltpu.VMEM((steps, 2, extent0, extent2), f32),
            pltpu.VMEM((steps, 4, 1, extent2), f32),
            pltpu.VMEM((steps, 4, 1, extent2), f32),
            pltpu.VMEM((n_span, 16, LANES), f32),
            pltpu.VMEM((n_stream, 16, LANES), f32),
            pltpu.SemaphoreType.DMA((4,)),
            pltpu.SemaphoreType.DMA((n_span,)),
            pltpu.SemaphoreType.DMA((n_span,)),
            pltpu.SemaphoreType.DMA((steps, 8)),
            pltpu.SemaphoreType.DMA((steps, 8)),
            pltpu.SemaphoreType.DMA((n_span,)),
            pltpu.SemaphoreType.DMA((n_span,)),
            pltpu.SemaphoreType.DMA((n_stream,)),
            pltpu.SemaphoreType.DMA((n_stream,)),
        ],
        compiler_params=pltpu.CompilerParams(
            collective_id=0, has_side_effects=True, vmem_limit_bytes=32 * 1024 * 1024
        ),
        cost_estimate=pl.CostEstimate(
            flops=6 * 10**9, bytes_accessed=4 * 2**20, transcendentals=10**4
        ),
        name="wind_farm_step",
    )(
        velocity.reshape(3, rows, extent2),
        coefficient.reshape(rows, extent2),
        coords,
        forces,
        line_id.reshape(1, points),
        line_gain.reshape(1, -1),
        dest_span.reshape(1, points),
        owner_element.reshape(1, points),
        *[jnp.asarray(table) for table in tables],
    )
    shape = (extent0, extent1, extent2)
    return pressure.reshape(shape), residual.reshape(shape)


def solution(mesh):
    return jax.shard_map(
        on_device,
        mesh=mesh,
        in_specs=(
            P(None, "stream", "span", None),
            P("stream", "span", None),
            P(None, ("stream", "span")),
            P(None, ("stream", "span")),
            P(("stream", "span")),
            P(),
            P(("stream", "span"), None),
            P(("stream", "span")),
        ),
        out_specs=(P("stream", "span", None), P("stream", "span", None)),
        check_vma=False,
    )
```

profile of v0, /device:TPU:0, one launch (start us, length us, event | category | flops | bytes accessed | tf_op | source)
XLA Modules:
  0.0 56.2 jit_solution(4255250407013549044)
XLA Ops:
  0.6 0.0 copy-start
  0.6 1.4 %copy-done = f32[3,8,16,1024]{3,2,1,0:T(8,128)S(1)} copy-done((f32[3,8,16,1024]{3,2,1,0:T(8,128)S(1)}, f32[3,8,16,1024]{3,2,1,0:T(8,128)}, u32[]{:S(2)}) %copy-start) | copy-done | bytes 1572888
  2.0 0.0 copy-start.1
  2.0 1.0 %copy-done.1 = f32[8,16,1024]{2,1,0:T(8,128)S(1)} copy-done((f32[8,16,1024]{2,1,0:T(8,128)S(1)}, f32[8,16,1024]{2,1,0:T(8,128)}, u32[]{:S(2)}) %copy-start.1) | copy-done | bytes 524312
  3.1 0.0 copy-start.2
  3.1 0.7 %copy-done.2 = f32[3,128]{1,0:T(4,128)S(1)} copy-done((f32[3,128]{1,0:T(4,128)S(1)}, f32[3,128]{1,0:T(4,128)}, u32[]{:S(2)}) %copy-start.2) | copy-done | bytes 1560
  3.8 0.0 copy-start.3
  3.8 0.7 %copy-done.3 = f32[3,128]{1,0:T(4,128)S(1)} copy-done((f32[3,128]{1,0:T(4,128)S(1)}, f32[3,128]{1,0:T(4,128)}, u32[]{:S(2)}) %copy-start.3) | copy-done | bytes 1560
  4.4 0.0 copy-start.4
  4.5 0.7 %copy-done.4 = f32[400]{0:T(512)S(1)} copy-done((f32[400]{0:T(512)S(1)}, f32[400]{0:T(512)}, u32[]{:S(2)}) %copy-start.4) | copy-done | bytes 1624
  5.1 0.0 copy-start.5
  5.1 0.7 %copy-done.5 = s32[128]{0:T(128)S(1)} copy-done((s32[128]{0:T(128)S(1)}, s32[128]{0:T(128)}, u32[]{:S(2)}) %copy-start.5) | copy-done | bytes 536
  5.8 0.0 copy-start.6
  5.8 0.7 %copy-done.6 = s32[128,1]{0,1:T(1,128)S(1)} copy-done((s32[128,1]{0,1:T(1,128)S(1)}, s32[128,1]{0,1:T(1,128)}, u32[]{:S(2)}) %copy-start.6) | copy-done | bytes 536
  6.4 0.0 copy-start.7
  6.4 0.7 %copy-done.7 = s32[128]{0:T(128)S(1)} copy-done((s32[128]{0:T(128)S(1)}, s32[128]{0:T(128)}, u32[]{:S(2)}) %copy-start.7) | copy-done | bytes 536
  7.1 0.0 copy-start.8
  7.1 1.0 %copy-done.8 = bf16[768,256]{1,0:T(8,128)(2,1)S(1)} copy-done((bf16[768,256]{1,0:T(8,128)(2,1)S(1)}, bf16[768,256]{1,0:T(8,128)(2,1)}, u32[]{:S(2)}) %copy-start.8) | copy-done | bytes 393240
  8.1 0.0 copy-start.9
  8.1 1.0 %copy-done.9 = bf16[768,256]{1,0:T(8,128)(2,1)S(1)} copy-done((bf16[768,256]{1,0:T(8,128)(2,1)S(1)}, bf16[768,256]{1,0:T(8,128)(2,1)}, u32[]{:S(2)}) %copy-start.9) | copy-done | bytes 393240
  9.1 0.0 copy-start.10
  9.1 0.9 %copy-done.10 = bf16[128,768]{1,0:T(8,128)(2,1)S(1)} copy-done((bf16[128,768]{1,0:T(8,128)(2,1)S(1)}, bf16[128,768]{1,0:T(8,128)(2,1)}, u32[]{:S(2)}) %copy-start.10) | copy-done | bytes 196632
  10.0 0.0 copy-start.11
  10.0 0.9 %copy-done.11 = bf16[256,384]{1,0:T(8,128)(2,1)S(1)} copy-done((bf16[256,384]{1,0:T(8,128)(2,1)S(1)}, bf16[256,384]{1,0:T(8,128)(2,1)}, u32[]{:S(2)}) %copy-start.11) | copy-done | bytes 196632
  10.9 0.0 copy-start.12
  10.9 0.9 %copy-done.12 = f32[128,256]{1,0:T(8,128)S(1)} copy-done((f32[128,256]{1,0:T(8,128)S(1)}, f32[128,256]{1,0:T(8,128)}, u32[]{:S(2)}) %copy-start.12) | copy-done | bytes 131096
  11.8 0.0 copy-start.13
  11.9 0.7 %copy-done.13 = f32[8,128]{1,0:T(8,128)S(1)} copy-done((f32[8,128]{1,0:T(8,128)S(1)}, f32[8,128]{1,0:T(8,128)}, u32[]{:S(2)}) %copy-start.13) | copy-done | bytes 4120
  12.5 42.0 %wind_farm_step.1 = (f32[128,1024]{1,0:T(8,128)S(1)}, f32[128,1024]{1,0:T(8,128)S(1)}) custom-call(f32[3,128,1024]{2,1,0:T(8,128)S(1)} %bitcast.10, f32[128,1024]{1,0:T(8,128)S(1)} %bitcast.11, f32[3,128]{1,0:T(4,128)S(1)} %copy-done.2, f32[3,128]{1,0:T(4,128)S(1)} %copy-done.3, s32[1,128]{1,0:T(1,128)S(1)} %bitcast.13, f32[1,400]{1,0:T(1,128)S(1)} %bitcast.12, ...), custom_call_target="tpu_custom_call" | custom-call | flops 6000000000 | bytes 4194304 | tf_op jit(solution)/shard_map/wind_farm_step/pallas_call | solution.py:590
  54.6 0.8 %copy.18 = f32[8,16,1024]{2,1,0:T(8,128)} copy(f32[8,16,1024]{2,1,0:T(8,128)S(1)} %bitcast.9) | data formatting | bytes 1048576
  55.4 0.8 %copy.19 = f32[8,16,1024]{2,1,0:T(8,128)} copy(f32[8,16,1024]{2,1,0:T(8,128)S(1)} %bitcast.8) | data formatting | bytes 1048576
Async XLA Ops:
  0.6 1.4 %copy-start = (f32[3,8,16,1024]{3,2,1,0:T(8,128)S(1)}, f32[3,8,16,1024]{3,2,1,0:T(8,128)}, u32[]{:S(2)}) copy-start(f32[3,8,16,1024]{3,2,1,0:T(8,128)} %param.14) | copy-start | bytes 4718596
  2.0 1.0 %copy-start.1 = (f32[8,16,1024]{2,1,0:T(8,128)S(1)}, f32[8,16,1024]{2,1,0:T(8,128)}, u32[]{:S(2)}) copy-start(f32[8,16,1024]{2,1,0:T(8,128)} %param.15) | copy-start | bytes 1572868
  3.1 0.7 %copy-start.2 = (f32[3,128]{1,0:T(4,128)S(1)}, f32[3,128]{1,0:T(4,128)}, u32[]{:S(2)}) copy-start(f32[3,128]{1,0:T(4,128)} %coords.1) | copy-start | bytes 4612
  3.8 0.7 %copy-start.3 = (f32[3,128]{1,0:T(4,128)S(1)}, f32[3,128]{1,0:T(4,128)}, u32[]{:S(2)}) copy-start(f32[3,128]{1,0:T(4,128)} %forces.1) | copy-start | bytes 4612
  4.4 0.7 %copy-start.4 = (f32[400]{0:T(512)S(1)}, f32[400]{0:T(512)}, u32[]{:S(2)}) copy-start(f32[400]{0:T(512)} %param.19) | copy-start | bytes 4804
  5.1 0.7 %copy-start.5 = (s32[128]{0:T(128)S(1)}, s32[128]{0:T(128)}, u32[]{:S(2)}) copy-start(s32[128]{0:T(128)} %param.18) | copy-start | bytes 1540
  5.8 0.7 %copy-start.6 = (s32[128,1]{0,1:T(1,128)S(1)}, s32[128,1]{0,1:T(1,128)}, u32[]{:S(2)}) copy-start(s32[128,1]{0,1:T(1,128)} %param.20) | copy-start | bytes 1540
  6.4 0.7 %copy-start.7 = (s32[128]{0:T(128)S(1)}, s32[128]{0:T(128)}, u32[]{:S(2)}) copy-start(s32[128]{0:T(128)} %param.21) | copy-start | bytes 1540
  7.1 1.0 %copy-start.8 = (bf16[768,256]{1,0:T(8,128)(2,1)S(1)}, bf16[768,256]{1,0:T(8,128)(2,1)}, u32[]{:S(2)}) copy-start(bf16[768,256]{1,0:T(8,128)(2,1)} %constant.15.clone.cols_bwd) | copy-start | bytes 1179652
  8.1 1.0 %copy-start.9 = (bf16[768,256]{1,0:T(8,128)(2,1)S(1)}, bf16[768,256]{1,0:T(8,128)(2,1)}, u32[]{:S(2)}) copy-start(bf16[768,256]{1,0:T(8,128)(2,1)} %constant.14.clone.cols_fwd) | copy-start | bytes 1179652
  9.1 0.9 %copy-start.10 = (bf16[128,768]{1,0:T(8,128)(2,1)S(1)}, bf16[128,768]{1,0:T(8,128)(2,1)}, u32[]{:S(2)}) copy-start(bf16[128,768]{1,0:T(8,128)(2,1)} %constant.13.clone.rows_bwd) | copy-start | bytes 589828
  10.0 0.9 %copy-start.11 = (bf16[256,384]{1,0:T(8,128)(2,1)S(1)}, bf16[256,384]{1,0:T(8,128)(2,1)}, u32[]{:S(2)}) copy-start(bf16[256,384]{1,0:T(8,128)(2,1)} %constant.12.clone.rows_fwd) | copy-start | bytes 589828
  10.9 0.9 %copy-start.12 = (f32[128,256]{1,0:T(8,128)S(1)}, f32[128,256]{1,0:T(8,128)}, u32[]{:S(2)}) copy-start(f32[128,256]{1,0:T(8,128)} %constant.16.clone.weight) | copy-start | bytes 393220
  11.8 0.7 %copy-start.13 = (f32[8,128]{1,0:T(8,128)S(1)}, f32[8,128]{1,0:T(8,128)}, u32[]{:S(2)}) copy-start(f32[8,128]{1,0:T(8,128)} %constant.17.clone.nodes) | copy-start | bytes 12292
where the time goes:
time: 56.7 us; the launch traced here: 56.2 us
  Pallas kernels  42 us (74%)
  local copies, waits for them, and re-layouts  13.5 us (24%)
  between operations  0.66 us (1%)
    pallas_call x1, Pallas kernels, on_device(): pl.pallas_call(functools.partial(body, sizes), out_shape=(block, block),...  42 us
    unnamed x30, local copies, waits for them, and re-layouts  13.5 us

commit v1 on v0

v1 whole, which is shorter than its diff:
```python
import functools

import jax
import jax.numpy as jnp
import numpy as np
from jax import lax
from jax.experimental import pallas as pl
from jax.experimental.pallas import tpu as pltpu
from jax.sharding import PartitionSpec as P

POLY = 8
ITERS = 3
LANES = 128
CHUNK = 256
PARTS = 2
N_IN = 14

kernel_width = 0.45
gll_nodes = [
    -1.0,
    -0.8717401485096066,
    -0.5917001814331423,
    -0.2092992179024789,
    0.2092992179024789,
    0.5917001814331423,
    0.8717401485096066,
    1.0,
]
MESH = pl.DeviceIdType.MESH
OFFSETS = [(1, 0), (-1, 0), (0, 1), (0, -1), (1, 1), (1, -1), (-1, 1), (-1, -1)]


def legendre_value(point, degree):
    previous = 1.0
    current = point
    for order in range(1, degree):
        following = ((2 * order + 1) * point * current - order * previous) / (order + 1)
        previous = current
        current = following
    return current


def gll_tables():
    degree = POLY - 1
    values = [legendre_value(point, degree) for point in gll_nodes]
    weights = [2.0 / (degree * (degree + 1) * value * value) for value in values]
    diffmat = np.zeros((POLY, POLY))
    for i in range(POLY):
        for j in range(POLY):
            if i != j:
                diffmat[i, j] = values[i] / (values[j] * (gll_nodes[i] - gll_nodes[j]))
    diffmat[0, 0] = -degree * (degree + 1) / 4.0
    diffmat[-1, -1] = degree * (degree + 1) / 4.0
    return (
        np.asarray(gll_nodes, np.float32),
        np.asarray(weights, np.float32),
        np.asarray(diffmat, np.float32),
    )


def constants(extent0, extent1):
    nodes, weights, diffmat = gll_tables()
    eye = functools.partial(np.eye, dtype=np.float32)
    along0 = np.kron(eye(extent0 // POLY), np.kron(diffmat, eye(extent1)))
    along1 = np.kron(eye(extent0 * extent1 // POLY), diffmat)
    rows = np.concatenate([along0, along1], axis=0)
    cols = np.kron(eye(CHUNK // POLY), diffmat)

    row_weight = np.kron(np.tile(weights, extent0 // POLY), np.tile(weights, extent1 // POLY))
    row_weight = row_weight.astype(np.float32)
    weight = row_weight[:, None] * np.tile(weights, CHUNK // POLY)[None, :]
    column = np.repeat(nodes[:, None], LANES, axis=1)
    return rows, rows.T.copy(), cols.T.copy(), cols, weight, column


def split2(value):
    high = value.astype(jnp.bfloat16)
    low = (value - high.astype(jnp.float32)).astype(jnp.bfloat16)
    return high, low


def split3(value):
    high = value.astype(jnp.bfloat16)
    rest = value - high.astype(jnp.float32)
    middle = rest.astype(jnp.bfloat16)
    low = (rest - middle.astype(jnp.float32)).astype(jnp.bfloat16)
    return high, middle, low


def dot(first, second):
    return jnp.dot(first, second, preferred_element_type=jnp.float32)


def dot_nt(first, second):
    return lax.dot_general(
        first, second, (((1,), (1,)), ((), ())), preferred_element_type=jnp.float32
    )


def stacked(value, axis):
    high, low = split2(value)
    return jnp.concatenate([high, low, high], axis=axis)


def combine(first, second, moments, shift):
    total = 0.0
    for i, x in enumerate(first):
        for j, y in enumerate(second):
            total = total + x * y * moments[i + j + shift]
    return total


def body(sizes, *refs):
    n_stream, n_span, extent0, extent1, extent2, capacity = sizes
    hbm_in, (pressure, residual) = refs[:N_IN], refs[N_IN : N_IN + 2]
    vmem_in = refs[N_IN + 2 : 2 * N_IN + 2]
    (
        rows_fwd,
        rows_bwd,
        cols_fwd,
        cols_bwd,
        basis,
        work,
        joined,
        out_pts,
        in_pts,
        lhs_pts,
        rhs_pts,
        recv_stream,
        send_span,
        recv_span,
        send_edge,
        recv_edge,
        sums1,
        sums2,
        load_sem,
        pts_send,
        pts_recv,
        halo_send,
        halo_recv,
        sum1_send,
        sum1_recv,
        sum2_send,
        sum2_recv,
    ) = refs[2 * N_IN + 2 :]
    (
        coords,
        forces,
        line_id,
        line_gain,
        dest_span,
        owner,
        nodes,
        rows_fwd_f32,
        rows_bwd_f32,
        cols_fwd_f32,
        cols_bwd_f32,
        weight,
        vel,
        metric,
    ) = vmem_in
    rows = extent0 * extent1
    me_s, me_p = lax.axis_index("stream"), lax.axis_index("span")

    def exists(offset):
        s, p = me_s + offset[0], me_p + offset[1]
        return (s >= 0) & (s < n_stream) & (p >= 0) & (p < n_span)

    def at_offset(offset):
        return (
            lax.rem(me_s + offset[0] + n_stream, n_stream),
            lax.rem(me_p + offset[1] + n_span, n_span),
        )

    span_peers = [lax.rem(me_p + j, n_span) for j in range(1, n_span)]
    stream_peers = [lax.rem(me_s + j, n_stream) for j in range(1, n_stream)]

    barrier = pltpu.get_barrier_semaphore()
    for peer in span_peers:
        pl.semaphore_signal(barrier, inc=1, device_id=(me_s, peer), device_id_type=MESH)
    for peer in stream_peers:
        pl.semaphore_signal(barrier, inc=1, device_id=(peer, me_p), device_id_type=MESH)
    greeted = n_span - 1 + n_stream - 1
    for offset in OFFSETS[4:]:

        @pl.when(exists(offset))
        def _(offset=offset):
            pl.semaphore_signal(
                barrier, inc=1, device_id=at_offset(offset), device_id_type=MESH
            )

        greeted = greeted + exists(offset).astype(jnp.int32)

    loads = [
        pltpu.make_async_copy(hbm_in[n], vmem_in[n], load_sem.at[n]) for n in range(N_IN)
    ]
    for load in loads:
        load.start()

    def from_offset(d):
        return exists((-OFFSETS[d][0], -OFFSETS[d][1]))

    for d in range(8):
        buffer = (recv_stream, recv_span, recv_edge)[0 if d < 2 else 1 if d < 4 else 2]
        at = d if d < 2 else d - 2 if d < 4 else d - 4

        @pl.when(jnp.logical_not(from_offset(d)))
        def _(buffer=buffer, at=at):
            for k in range(ITERS + 1):
                buffer[k, at] = jnp.zeros(buffer.shape[2:], jnp.float32)

    points = coords.shape[1]
    group = LANES // capacity
    groups = n_span // group
    lines = line_gain.shape[1]
    earlier = (
        lax.broadcasted_iota(jnp.int32, (points, points), 0)
        < lax.broadcasted_iota(jnp.int32, (points, points), 1)
    ).astype(jnp.bfloat16)
    for load in loads[:7]:
        load.wait()
    ids = line_id[...]
    chosen = (lax.broadcasted_iota(jnp.int32, (lines, points), 0) == ids).astype(jnp.bfloat16)
    gain = sum(dot(part, chosen) for part in reversed(split3(line_gain[...])))
    scaled = forces[...] * gain
    target = dest_span[...]
    spans_at = lax.broadcasted_iota(jnp.int32, (n_span, points), 0)
    named = (spans_at == target).astype(jnp.float32)
    before = dot(named.astype(jnp.bfloat16), earlier)
    rank = jnp.sum(named * before, axis=0, keepdims=True).astype(jnp.int32)
    slot = target * LANES + lax.rem(me_p, group) * capacity + rank
    payload = jnp.concatenate(
        [
            coords[...],
            scaled,
            owner[...].astype(jnp.float32),
            jnp.zeros((1, points), jnp.float32),
        ],
        axis=0,
    )
    parts = jnp.concatenate(
        [p.astype(jnp.float32) for p in split3(payload)], axis=0
    ).astype(jnp.bfloat16)
    for dest in range(n_span):
        placed = (
            lax.broadcasted_iota(jnp.int32, (LANES, points), 0) + dest * LANES == slot
        ).astype(jnp.float32).astype(jnp.bfloat16)
        tile = dot_nt(parts, placed)
        out_pts[dest] = (tile[16:24] + tile[8:16]) + tile[0:8]

    for load in loads[7:12]:
        load.wait()
    high, low = split2(rows_fwd_f32[...])
    rows_fwd[...] = jnp.concatenate([high, high, low, low], axis=1)
    high, low = split2(rows_bwd_f32[...])
    rows_bwd[...] = jnp.concatenate([high, high, low], axis=1)
    for matrix, out in ((cols_fwd_f32, cols_fwd), (cols_bwd_f32, cols_bwd)):
        high, low = split2(matrix[...])
        out[...] = jnp.concatenate([high, high, low], axis=0)

    pl.semaphore_wait(barrier, greeted)

    def points_copy(peer, slot_at):
        return pltpu.make_async_remote_copy(
            src_ref=out_pts.at[peer],
            dst_ref=in_pts.at[slot_at],
            send_sem=pts_send.at[peer],
            recv_sem=pts_recv.at[slot_at],
            device_id=(me_s, peer),
            device_id_type=MESH,
        )

    for peer in span_peers:
        points_copy(peer, me_p).start()
    in_pts[me_p] = out_pts[me_p]

    chunks = [slice(c, c + CHUNK) for c in range(0, extent2, CHUNK)]
    for load in loads[12:]:
        load.wait()
    for cols in chunks:
        metric[:, cols] = metric[:, cols] * weight[...]

    for peer in span_peers:
        points_copy(peer, peer).wait_recv()

    elems2 = extent2 // POLY
    node_col = nodes[...]
    for g in range(groups):
        tile = in_pts[g * group]
        for i in range(1, group):
            tile = tile + in_pts[g * group + i]
        lanes = slice(g * LANES, (g + 1) * LANES)
        kern = [
            jnp.exp(-(((node_col - tile[k : k + 1]) / kernel_width) ** 2)) for k in range(3)
        ]
        elem = tile[6:7].astype(jnp.int32)
        elem_y = lax.rem(lax.div(elem, elems2), extent1 // POLY)
        elem_x = lax.div(elem, elems2 * (extent1 // POLY))
        elem_z = lax.rem(elem, elems2)
        for c in range(3):
            for a in range(extent0):
                for ey in range(extent1 // POLY):
                    mine = (elem_x == a // POLY) & (elem_y == ey)
                    factor = tile[3 + c : 4 + c] * kern[0][a % POLY : a % POLY + 1]
                    base = c * rows + a * extent1 + ey * POLY
                    lhs_pts[base : base + POLY, lanes] = jnp.where(mine, factor, 0.0) * kern[1]
        for ez in range(elems2):
            rhs_pts[ez * POLY : (ez + 1) * POLY, lanes] = jnp.where(elem_z == ez, kern[2], 0.0)

    left_pts = stacked(lhs_pts[...], 1)

    def tile_sum(value):
        total = jnp.sum(value.reshape(rows // POLY, POLY, CHUNK), axis=0)
        return sum(total[:, at : at + LANES] for at in range(0, CHUNK, LANES))

    def rhs_chunk(cols):
        high, low = split2(rhs_pts[cols, :])
        force = dot_nt(left_pts, jnp.concatenate([high, high, low], axis=1))
        part = [
            weight[...] * (vel[c, :, cols] + force[c * rows : (c + 1) * rows]) for c in range(3)
        ]
        both = jnp.concatenate(part[:2], axis=0)
        work[0, :, cols] = dot(rows_bwd[...], stacked(both, 0)) + dot(
            stacked(part[2], 1), cols_bwd[...]
        )

    def operator_chunk(k, cols):
        field = basis[k, :, cols]
        high, low = split2(field)
        m = metric[:, cols]
        grad = dot(rows_fwd[...], jnp.concatenate([high, low, high, low], axis=0))
        grad2 = dot(jnp.concatenate([high, low, high], axis=1), cols_fwd[...])
        both = jnp.concatenate([grad[:rows] * m, grad[rows:] * m], axis=0)
        out = (
            dot(rows_bwd[...], stacked(both, 0))
            + dot(stacked(grad2 * m, 1), cols_bwd[...])
            + weight[...] * field
        )
        work[k + 1, :, cols] = out
        return tile_sum(field * work[k, :, cols]), tile_sum(field * out)

    last0, last1 = extent0 - 1, extent1 - 1
    part_width = extent2 // PARTS

    def halo_copy(k, d, q):
        cols = pl.ds(q * part_width, part_width)
        if d < 2:
            src = work.at[k, pl.ds(last0 * extent1 if d == 0 else 0, extent1), cols]
            dst = recv_stream.at[k, d, :, cols]
        elif d < 4:
            src, dst = send_span.at[k, d - 2, :, cols], recv_span.at[k, d - 2, :, cols]
        else:
            src, dst = send_edge.at[k, d - 4, :, cols], recv_edge.at[k, d - 4, :, cols]
        return pltpu.make_async_remote_copy(
            src_ref=src,
            dst_ref=dst,
            send_sem=halo_send.at[k, d, q],
            recv_sem=halo_recv.at[k, d, q],
            device_id=at_offset(OFFSETS[d]),
            device_id_type=MESH,
        )

    def send_faces(k, q):
        cols = slice(q * part_width, (q + 1) * part_width)
        for a in range(extent0):
            top = work[k, a * extent1 + last1 : a * extent1 + last1 + 1, cols]
            bottom = work[k, a * extent1 : a * extent1 + 1, cols]
            send_span[k, 0, a : a + 1, cols] = top
            send_span[k, 1, a : a + 1, cols] = bottom
            if a == last0:
                send_edge[k, 0, :, cols] = top
                send_edge[k, 1, :, cols] = bottom
            if a == 0:
                send_edge[k, 2, :, cols] = top
                send_edge[k, 3, :, cols] = bottom
        for d in range(8):

            @pl.when(exists(OFFSETS[d]))
            def _(d=d):
                halo_copy(k, d, q).start()

    def join(k, q):
        for d in (2, 3, 4, 5, 6, 7, 0, 1):

            @pl.when(from_offset(d))
            def _(d=d):
                halo_copy(k, d, q).wait_recv()

        cols = slice(q * part_width, (q + 1) * part_width)
        sub = lax.broadcasted_iota(jnp.int32, (POLY, part_width), 0)
        for a in range(extent0):
            tiles = []
            for ey in range(extent1 // POLY):
                base = a * extent1 + ey * POLY
                x = work[k, base : base + POLY, cols]
                if a == 0:
                    x = x + recv_stream[k, 0, ey * POLY : (ey + 1) * POLY, cols]
                if a == last0:
                    x = x + recv_stream[k, 1, ey * POLY : (ey + 1) * POLY, cols]
                tiles.append(x)
            lower = recv_span[k, 0, a : a + 1, cols]
            upper = recv_span[k, 1, a : a + 1, cols]
            if a == 0:
                lower = lower + recv_edge[k, 0, :, cols]
                upper = upper + recv_edge[k, 1, :, cols]
            if a == last0:
                lower = lower + recv_edge[k, 2, :, cols]
                upper = upper + recv_edge[k, 3, :, cols]
            for ey, x in enumerate(tiles):
                below = lower if ey == 0 else pltpu.roll(tiles[ey - 1], 1, 0)
                above = upper if ey + 1 == len(tiles) else pltpu.roll(tiles[ey + 1], POLY - 1, 0)
                base = a * extent1 + ey * POLY
                joined[base : base + POLY, cols] = (
                    x + jnp.where(sub == 0, below, 0.0) + jnp.where(sub == POLY - 1, above, 0.0)
                )

    def assemble(k, cols):
        start, stop = max(cols.start - LANES, 0), min(cols.stop + LANES, extent2)
        width = stop - start
        lane = lax.broadcasted_iota(jnp.int32, (POLY, CHUNK), 1) + cols.start
        first2 = (lane % POLY == 0) & (lane > 0)
        last2 = (lane % POLY == POLY - 1) & (lane < extent2 - 1)
        inner = slice(cols.start - start, cols.stop - start)
        for base in range(0, rows, POLY):
            x = joined[base : base + POLY, start:stop]
            lower = pltpu.roll(x, 1, 1)[:, inner]
            upper = pltpu.roll(x, width - 1, 1)[:, inner]
            basis[k, base : base + POLY, cols] = (
                x[:, inner] + jnp.where(first2, lower, 0.0) + jnp.where(last2, upper, 0.0)
            )

    per_part = len(chunks) // PARTS

    def joined_chunks(k):
        have = 0
        for n, cols in enumerate(chunks):
            need = min((n + 1) // per_part + 1, PARTS)
            while have < need:
                join(k, have)
                have += 1
            assemble(k, cols)
            yield n, cols

    for n, cols in enumerate(chunks):
        rhs_chunk(cols)
        if (n + 1) % per_part == 0:
            send_faces(0, n // per_part)
    mine = []
    for k in range(ITERS):
        even = odd = 0.0
        for n, cols in joined_chunks(k):
            more = operator_chunk(k, cols)
            even, odd = even + more[0], odd + more[1]
            if (n + 1) % per_part == 0:
                send_faces(k + 1, n // per_part)
        mine += [even, odd]

    mine = [jnp.sum(total, axis=0, keepdims=True) for total in mine]
    mine.append(jnp.zeros((8 - len(mine), LANES), jnp.float32))
    sums1[me_p] = jnp.concatenate(mine, axis=0)

    def sum1_copy(peer, slot_at):
        return pltpu.make_async_remote_copy(
            src_ref=sums1.at[me_p],
            dst_ref=sums1.at[slot_at],
            send_sem=sum1_send.at[peer],
            recv_sem=sum1_recv.at[slot_at],
            device_id=(me_s, peer),
            device_id_type=MESH,
        )

    def sum2_copy(peer, slot_at):
        return pltpu.make_async_remote_copy(
            src_ref=sums2.at[me_s],
            dst_ref=sums2.at[slot_at],
            send_sem=sum2_send.at[peer],
            recv_sem=sum2_recv.at[slot_at],
            device_id=(peer, me_p),
            device_id_type=MESH,
        )

    for peer in span_peers:
        sum1_copy(peer, me_p).start()
    for peer in span_peers:
        sum1_copy(peer, peer).wait_recv()
    total = sums1[0]
    for i in range(1, n_span):
        total = total + sums1[i]
    sums2[me_s] = total
    for peer in stream_peers:
        sum2_copy(peer, me_s).start()
    for _ in joined_chunks(ITERS):
        pass
    for peer in stream_peers:
        sum2_copy(peer, peer).wait_recv()
    total = sums2[0]
    for i in range(1, n_stream):
        total = total + sums2[i]
    total = jnp.broadcast_to(jnp.sum(total, axis=1, keepdims=True), (8, LANES))
    moments = [total[n : n + 1] for n in range(2 * ITERS)]

    one = jnp.ones((1, LANES), jnp.float32)
    res, direction, pres = [one], [one], [0.0] * ITERS
    norm = moments[0]
    for iteration in range(ITERS):
        step_len = norm / combine(direction, direction, moments, 1)
        for i, x in enumerate(direction):
            pres[i] = pres[i] + step_len * x
        res = res + [0.0]
        res = [res[0]] + [x - step_len * y for x, y in zip(res[1:], direction)]
        if iteration + 1 < ITERS:
            norm_next = combine(res, res, moments, 0)
            ratio = norm_next / norm
            direction = [x + ratio * y for x, y in zip(res, direction + [0.0])]
            norm = norm_next

    pres = [jnp.broadcast_to(x[:, 0:1], (POLY, extent2)) for x in pres]
    res = [jnp.broadcast_to(x[:, 0:1], (POLY, extent2)) for x in res]

    def finish(step, carry):
        at = pl.ds(pl.multiple_of(step * POLY, POLY), POLY)
        vec = [basis[i, at, :] for i in range(ITERS + 1)]
        out = pres[0] * vec[0]
        for i in range(1, ITERS):
            out = out + pres[i] * vec[i]
        pressure[at, :] = out
        out = res[0] * vec[0]
        for i in range(1, ITERS + 1):
            out = out + res[i] * vec[i]
        residual[at, :] = out
        return carry

    lax.fori_loop(0, rows // POLY, finish, 0)

    for peer in span_peers:
        points_copy(peer, me_p).wait_send()
        sum1_copy(peer, me_p).wait_send()
    for peer in stream_peers:
        sum2_copy(peer, me_s).wait_send()
    for d in range(8):

        @pl.when(exists(OFFSETS[d]))
        def _(d=d):
            for k in range(ITERS + 1):
                for q in range(PARTS):
                    halo_copy(k, d, q).wait_send()


def on_device(velocity, coefficient, coords, forces, line_id, line_gain, dest_span, owner_element):
    extent0, extent1, extent2 = coefficient.shape
    rows = extent0 * extent1
    points = coords.shape[1]
    n_stream, n_span = lax.axis_size("stream"), lax.axis_size("span")
    capacity = max(2, 2 * points // n_span)
    total_pts = n_span * capacity
    tables = constants(extent0, extent1)
    f32 = jnp.float32
    block = jax.ShapeDtypeStruct((rows, extent2), f32)
    vmem = pl.BlockSpec(memory_space=pltpu.VMEM)
    hbm = pl.BlockSpec(memory_space=pl.ANY)
    steps = ITERS + 1
    sizes = (n_stream, n_span, extent0, extent1, extent2, capacity)
    rows_fwd, rows_bwd, cols_fwd, cols_bwd, weight, column = [jnp.asarray(x) for x in tables]
    operands = [
        coords,
        forces,
        line_id.reshape(1, points),
        line_gain.reshape(1, -1),
        dest_span.reshape(1, points),
        owner_element.reshape(1, points),
        column,
        rows_fwd,
        rows_bwd,
        cols_fwd,
        cols_bwd,
        weight,
        velocity.reshape(3, rows, extent2),
        coefficient.reshape(rows, extent2),
    ]
    pressure, residual = pl.pallas_call(
        functools.partial(body, sizes),
        out_shape=(block, block),
        in_specs=[hbm] * N_IN,
        out_specs=(vmem, vmem),
        scratch_shapes=[pltpu.VMEM(x.shape, x.dtype) for x in operands]
        + [
            pltpu.VMEM((2 * rows, 4 * rows), jnp.bfloat16),
            pltpu.VMEM((rows, 6 * rows), jnp.bfloat16),
            pltpu.VMEM((3 * CHUNK, CHUNK), jnp.bfloat16),
            pltpu.VMEM((3 * CHUNK, CHUNK), jnp.bfloat16),
            pltpu.VMEM((steps, rows, extent2), f32),
            pltpu.VMEM((steps, rows, extent2), f32),
            pltpu.VMEM((rows, extent2), f32),
            pltpu.VMEM((n_span, 8, LANES), f32),
            pltpu.VMEM((n_span, 8, LANES), f32),
            pltpu.VMEM((3 * rows, total_pts), f32),
            pltpu.VMEM((extent2, total_pts), f32),
            pltpu.VMEM((steps, 2, extent1, extent2), f32),
            pltpu.VMEM((steps, 2, extent0, extent2), f32),
            pltpu.VMEM((steps, 2, extent0, extent2), f32),
            pltpu.VMEM((steps, 4, 1, extent2), f32),
            pltpu.VMEM((steps, 4, 1, extent2), f32),
            pltpu.VMEM((n_span, 8, LANES), f32),
            pltpu.VMEM((n_stream, 8, LANES), f32),
            pltpu.SemaphoreType.DMA((N_IN,)),
            pltpu.SemaphoreType.DMA((n_span,)),
            pltpu.SemaphoreType.DMA((n_span,)),
            pltpu.SemaphoreType.DMA((steps, 8, PARTS)),
            pltpu.SemaphoreType.DMA((steps, 8, PARTS)),
            pltpu.SemaphoreType.DMA((n_span,)),
            pltpu.SemaphoreType.DMA((n_span,)),
            pltpu.SemaphoreType.DMA((n_stream,)),
            pltpu.SemaphoreType.DMA((n_stream,)),
        ],
        compiler_params=pltpu.CompilerParams(
            collective_id=0, has_side_effects=True, vmem_limit_bytes=60 * 1024 * 1024
        ),
        cost_estimate=pl.CostEstimate(
            flops=6 * 10**9, bytes_accessed=4 * 2**20, transcendentals=10**4
        ),
        name="wind_farm_step",
    )(*operands)
    shape = (extent0, extent1, extent2)
    return pressure.reshape(shape), residual.reshape(shape)


def solution(mesh):
    return jax.shard_map(
        on_device,
        mesh=mesh,
        in_specs=(
            P(None, "stream", "span", None),
            P("stream", "span", None),
            P(None, ("stream", "span")),
            P(None, ("stream", "span")),
            P(("stream", "span")),
            P(),
            P(("stream", "span"), None),
            P(("stream", "span")),
        ),
        out_specs=(P("stream", "span", None), P("stream", "span", None)),
        check_vma=False,
    )
```

time: 56.7 us -> 41.8 us (0.74)
  local copies, waits for them, and re-layouts: 13.5 us -> 3.77 us
  Pallas kernels: 42 us -> 37.1 us
    unnamed x30 -> x2, local copies, waits for them, and re-layouts: 13.5 us -> 3.77 us
    pallas_call x1, Pallas kernels: 42 us -> 37.1 us  [on_device(): pl.pallas_call(functools.partial(body, sizes), out_shape=(block, block),...]
where the time goes in v1:
time: 41.8 us; the launch traced here: 41.5 us
  Pallas kernels  37.1 us (89%)
  local copies, waits for them, and re-layouts  3.77 us (9%)
  between operations  0.64 us (2%)
    pallas_call x1, Pallas kernels, on_device(): pl.pallas_call(functools.partial(body, sizes), out_shape=(block, block),...  37.1 us
    unnamed x2, local copies, waits for them, and re-layouts  3.77 us

profile of v1, /device:TPU:0, one launch (start us, length us, event | category | flops | bytes accessed | tf_op | source)
XLA Modules:
  0.0 41.5 jit_solution(6652652768053259371)
XLA Ops:
  0.6 37.1 %wind_farm_step.1 = (f32[128,1024]{1,0:T(8,128)}, f32[128,1024]{1,0:T(8,128)}) custom-call(f32[3,128]{1,0:T(4,128)} %refs_0_.1, f32[3,128]{1,0:T(4,128)} %refs_1_.1, s32[1,128]{1,0:T(1,128)} %bitcast.13, f32[1,400]{1,0:T(1,128)} %bitcast.12, s32[1,128]{1,0:T(1,128)} %bitcast.14, s32[1,128]{1,0:T(1,128)} %bitcast.15, f32[8,128]{1,0:T(8,128)} %constant.17.clone.refs_6_, ...), custom_call_target="tpu_custom_call" | custom-call | flops 6000000000 | bytes 4194304 | tf_op jit(solution)/shard_map/wind_farm_step/pallas_call | solution.py:580
  37.8 1.9 %copy.18 = f32[8,16,1024]{2,1,0:T(8,128)} copy(f32[8,16,1024]{2,1,0:T(8,128)} %bitcast.9) | data formatting | bytes 1048576
  39.6 1.9 %copy.19 = f32[8,16,1024]{2,1,0:T(8,128)} copy(f32[8,16,1024]{2,1,0:T(8,128)} %bitcast.8) | data formatting | bytes 1048576

commit v2 on v1

--- a/solution.py
+++ b/solution.py
@@ -69,7 +69,8 @@
     row_weight = np.kron(np.tile(weights, extent0 // POLY), np.tile(weights, extent1 // POLY))
     row_weight = row_weight.astype(np.float32)
     weight = row_weight[:, None] * np.tile(weights, CHUNK // POLY)[None, :]
-    column = np.repeat(nodes[:, None], LANES, axis=1)
+    table = np.concatenate([nodes[:, None], weights[:, None], diffmat.T * weights[None, :]], axis=1)
+    column = np.repeat(table.T.reshape(-1, 1), LANES, axis=1)
     return rows, rows.T.copy(), cols.T.copy(), cols, weight, column
 
 
@@ -112,8 +113,10 @@
 
 def body(sizes, *refs):
     n_stream, n_span, extent0, extent1, extent2, capacity = sizes
-    hbm_in, (pressure, residual) = refs[:N_IN], refs[N_IN : N_IN + 2]
-    vmem_in = refs[N_IN + 2 : 2 * N_IN + 2]
+    n_out = 3 * ITERS + 2
+    hbm_in, outs = refs[:N_IN], refs[N_IN : N_IN + n_out]
+    basis_out, factors = outs[: ITERS + 1], outs[ITERS + 1 :]
+    vmem_in = refs[N_IN + n_out : 2 * N_IN + n_out]
     (
         rows_fwd,
         rows_bwd,
@@ -134,6 +137,7 @@
         sums1,
         sums2,
         load_sem,
+        store_sem,
         pts_send,
         pts_recv,
         halo_send,
@@ -142,7 +146,7 @@
         sum1_recv,
         sum2_send,
         sum2_recv,
-    ) = refs[2 * N_IN + 2 :]
+    ) = refs[2 * N_IN + n_out :]
     (
         coords,
         forces,
@@ -278,34 +282,50 @@
     for load in loads[12:]:
         load.wait()
     for cols in chunks:
-        metric[:, cols] = metric[:, cols] * weight[...]
+        w = weight[...]
+        both = jnp.concatenate([w * vel[0, :, cols], w * vel[1, :, cols]], axis=0)
+        work[0, :, cols] = dot(rows_bwd[...], stacked(both, 0)) + dot(
+            stacked(w * vel[2, :, cols], 1), cols_bwd[...]
+        )
+        metric[:, cols] = metric[:, cols] * w
 
     for peer in span_peers:
         points_copy(peer, peer).wait_recv()
 
     elems2 = extent2 // POLY
-    node_col = nodes[...]
+    total_pts = groups * LANES
+    node_col = nodes[0:POLY]
+    weight_col = nodes[POLY : 2 * POLY]
+    diff_cols = [nodes[(2 + a) * POLY : (3 + a) * POLY] for a in range(POLY)]
     for g in range(groups):
         tile = in_pts[g * group]
         for i in range(1, group):
             tile = tile + in_pts[g * group + i]
         lanes = slice(g * LANES, (g + 1) * LANES)
-        kern = [
-            jnp.exp(-(((node_col - tile[k : k + 1]) / kernel_width) ** 2)) for k in range(3)
-        ]
+        lanes_diff = slice(total_pts + g * LANES, total_pts + (g + 1) * LANES)
+        plain, diff = [], []
+        for k in range(3):
+            kern = jnp.exp(-(((node_col - tile[k : k + 1]) / kernel_width) ** 2))
+            plain.append(weight_col * kern)
+            diff.append(sum(diff_cols[a] * kern[a : a + 1] for a in range(POLY)))
         elem = tile[6:7].astype(jnp.int32)
         elem_y = lax.rem(lax.div(elem, elems2), extent1 // POLY)
         elem_x = lax.div(elem, elems2 * (extent1 // POLY))
         elem_z = lax.rem(elem, elems2)
-        for c in range(3):
-            for a in range(extent0):
-                for ey in range(extent1 // POLY):
-                    mine = (elem_x == a // POLY) & (elem_y == ey)
-                    factor = tile[3 + c : 4 + c] * kern[0][a % POLY : a % POLY + 1]
-                    base = c * rows + a * extent1 + ey * POLY
-                    lhs_pts[base : base + POLY, lanes] = jnp.where(mine, factor, 0.0) * kern[1]
+        for a in range(extent0):
+            for ey in range(extent1 // POLY):
+                mine = (elem_x == a // POLY) & (elem_y == ey)
+                at = slice(a % POLY, a % POLY + 1)
+                factor0 = jnp.where(mine, tile[3:4] * diff[0][at], 0.0)
+                factor1 = jnp.where(mine, tile[4:5] * plain[0][at], 0.0)
+                factor2 = jnp.where(mine, tile[5:6] * plain[0][at], 0.0)
+                base = a * extent1 + ey * POLY
+                lhs_pts[base : base + POLY, lanes] = factor0 * plain[1] + factor1 * diff[1]
+                lhs_pts[base : base + POLY, lanes_diff] = factor2 * plain[1]
         for ez in range(elems2):
-            rhs_pts[ez * POLY : (ez + 1) * POLY, lanes] = jnp.where(elem_z == ez, kern[2], 0.0)
+            at = slice(ez * POLY, (ez + 1) * POLY)
+            rhs_pts[at, lanes] = jnp.where(elem_z == ez, plain[2], 0.0)
+            rhs_pts[at, lanes_diff] = jnp.where(elem_z == ez, diff[2], 0.0)
 
     left_pts = stacked(lhs_pts[...], 1)
 
@@ -316,13 +336,7 @@
     def rhs_chunk(cols):
         high, low = split2(rhs_pts[cols, :])
         force = dot_nt(left_pts, jnp.concatenate([high, high, low], axis=1))
-        part = [
-            weight[...] * (vel[c, :, cols] + force[c * rows : (c + 1) * rows]) for c in range(3)
-        ]
-        both = jnp.concatenate(part[:2], axis=0)
-        work[0, :, cols] = dot(rows_bwd[...], stacked(both, 0)) + dot(
-            stacked(part[2], 1), cols_bwd[...]
-        )
+        work[0, :, cols] = work[0, :, cols] + force
 
     def operator_chunk(k, cols):
         field = basis[k, :, cols]
@@ -431,6 +445,9 @@
 
     per_part = len(chunks) // PARTS
 
+    def store(k):
+        return pltpu.make_async_copy(basis.at[k], basis_out[k], store_sem.at[k])
+
     def joined_chunks(k):
         have = 0
         for n, cols in enumerate(chunks):
@@ -439,6 +456,8 @@
                 join(k, have)
                 have += 1
             assemble(k, cols)
+            if n + 1 == len(chunks):
+                store(k).start()
             yield n, cols
 
     for n, cols in enumerate(chunks):
@@ -514,24 +533,11 @@
             direction = [x + ratio * y for x, y in zip(res, direction + [0.0])]
             norm = norm_next
 
-    pres = [jnp.broadcast_to(x[:, 0:1], (POLY, extent2)) for x in pres]
-    res = [jnp.broadcast_to(x[:, 0:1], (POLY, extent2)) for x in res]
-
-    def finish(step, carry):
-        at = pl.ds(pl.multiple_of(step * POLY, POLY), POLY)
-        vec = [basis[i, at, :] for i in range(ITERS + 1)]
-        out = pres[0] * vec[0]
-        for i in range(1, ITERS):
-            out = out + pres[i] * vec[i]
-        pressure[at, :] = out
-        out = res[0] * vec[0]
-        for i in range(1, ITERS + 1):
-            out = out + res[i] * vec[i]
-        residual[at, :] = out
-        return carry
-
-    lax.fori_loop(0, rows // POLY, finish, 0)
-
+    for factor, value in zip(factors, pres + res):
+        factor[...] = value[:, 0:1]
+
+    for k in range(ITERS + 1):
+        store(k).wait()
     for peer in span_peers:
         points_copy(peer, me_p).wait_send()
         sum1_copy(peer, me_p).wait_send()
@@ -577,11 +583,11 @@
         velocity.reshape(3, rows, extent2),
         coefficient.reshape(rows, extent2),
     ]
-    pressure, residual = pl.pallas_call(
+    outs = pl.pallas_call(
         functools.partial(body, sizes),
-        out_shape=(block, block),
+        out_shape=(block,) * steps + (jax.ShapeDtypeStruct((1, 1), f32),) * (2 * ITERS + 1),
         in_specs=[hbm] * N_IN,
-        out_specs=(vmem, vmem),
+        out_specs=(hbm,) * steps + (vmem,) * (2 * ITERS + 1),
         scratch_shapes=[pltpu.VMEM(x.shape, x.dtype) for x in operands]
         + [
             pltpu.VMEM((2 * rows, 4 * rows), jnp.bfloat16),
@@ -593,8 +599,8 @@
             pltpu.VMEM((rows, extent2), f32),
             pltpu.VMEM((n_span, 8, LANES), f32),
             pltpu.VMEM((n_span, 8, LANES), f32),
-            pltpu.VMEM((3 * rows, total_pts), f32),
-            pltpu.VMEM((extent2, total_pts), f32),
+            pltpu.VMEM((rows, 2 * total_pts), f32),
+            pltpu.VMEM((extent2, 2 * total_pts), f32),
             pltpu.VMEM((steps, 2, extent1, extent2), f32),
             pltpu.VMEM((steps, 2, extent0, extent2), f32),
             pltpu.VMEM((steps, 2, extent0, extent2), f32),
@@ -603,6 +609,7 @@
             pltpu.VMEM((n_span, 8, LANES), f32),
             pltpu.VMEM((n_stream, 8, LANES), f32),
             pltpu.SemaphoreType.DMA((N_IN,)),
+            pltpu.SemaphoreType.DMA((steps,)),
             pltpu.SemaphoreType.DMA((n_span,)),
             pltpu.SemaphoreType.DMA((n_span,)),
             pltpu.SemaphoreType.DMA((steps, 8, PARTS)),
@@ -621,7 +628,11 @@
         name="wind_farm_step",
     )(*operands)
     shape = (extent0, extent1, extent2)
-    return pressure.reshape(shape), residual.reshape(shape)
+    basis = [vector.reshape(shape) for vector in outs[:steps]]
+    factors = [factor.reshape(()) for factor in outs[steps:]]
+    pressure = sum(factors[i] * basis[i] for i in range(ITERS))
+    residual = sum(factors[ITERS + i] * basis[i] for i in range(steps))
+    return pressure, residual
 
 
 def solution(mesh):

time: 41.8 us -> 43.4 us (1.038)
  other arithmetic: 0 us -> 7.1 us
  local copies, waits for them, and re-layouts: 3.77 us -> 0 us
  Pallas kernels: 37.1 us -> 35.5 us
    add x0 -> x1, other arithmetic: none -> 7.1 us  [on_device(): residual = sum((factors[ITERS + i] * basis[i] for i in range(steps)))]
    unnamed x2 -> x0, local copies, waits for them, and re-layouts: 3.77 us -> none
    pallas_call x1, Pallas kernels: 37.1 us -> 35.5 us  [on_device(): pl.pallas_call(functools.partial(body, sizes), out_shape=(block,) * steps...]
where the time goes in v2:
time: 43.4 us; the launch traced here: 43.2 us
  Pallas kernels  35.5 us (82%)
  other arithmetic  7.1 us (16%)
  between operations  0.64 us (1%)
    pallas_call x1, Pallas kernels, on_device(): pl.pallas_call(functools.partial(body, sizes), out_shape=(block,) * steps...  35.5 us
    add x1, other arithmetic, on_device(): residual = sum((factors[ITERS + i] * basis[i] for i in range(steps)))  7.1 us

profile of v2, /device:TPU:0, one launch (start us, length us, event | category | flops | bytes accessed | tf_op | source)
XLA Modules:
  0.0 43.2 jit_solution(6410791021127615708)
XLA Ops:
  0.6 35.5 %wind_farm_step.1 = (f32[128,1024]{1,0:T(8,128)}, f32[128,1024]{1,0:T(8,128)}, f32[128,1024]{1,0:T(8,128)}, f32[128,1024]{1,0:T(8,128)}, f32[1,1]{1,0:T(1,128)},...) custom-call(f32[3,128]{1,0:T(4,128)} %refs_0_.1, ...), custom_call_target="tpu_custom_call" | custom-call | flops 6000000000 | bytes 4194304 | tf_op jit(solution)/shard_map/wind_farm_step/pallas_call | solution.py:586
  36.1 7.1 %multiply_add_fusion = (f32[128,1024]{1,0:T(8,128)}, f32[128,1024]{1,0:T(8,128)}) fusion(f32[128,1024]{1,0:T(8,128)} %get-tuple-element.23, f32[128,1024]{1,0:T(8,128)} %get-tuple-element.18, f32[128,1024]{1,0:T(8,128)} %get-tuple-element.16, f32[128,1024]{1,0:T(8,128)} %get-tuple-element.14, f32[]{:T(128)} %bitcast.13, f32[]{:T(128)} %bitcast.12, f32[]{:T(128)} %bitcast.11, ...), kind=kLoop, calls=%fused_computation | loop fusion | flops 1572864 | bytes 3145756 | tf_op jit(solution)/shard_map/add | solution.py:634

commit v3 on v2

--- a/solution.py
+++ b/solution.py
@@ -12,7 +12,7 @@
 ITERS = 3
 LANES = 128
 CHUNK = 256
-PARTS = 2
+PARTS = 4
 N_IN = 14
 
 kernel_width = 0.45
@@ -113,9 +113,9 @@
 
 def body(sizes, *refs):
     n_stream, n_span, extent0, extent1, extent2, capacity = sizes
-    n_out = 3 * ITERS + 2
+    n_out = ITERS + 2
     hbm_in, outs = refs[:N_IN], refs[N_IN : N_IN + n_out]
-    basis_out, factors = outs[: ITERS + 1], outs[ITERS + 1 :]
+    basis_out, factors = outs[: ITERS + 1], outs[ITERS + 1]
     vmem_in = refs[N_IN + n_out : 2 * N_IN + n_out]
     (
         rows_fwd,
@@ -252,6 +252,22 @@
         tile = dot_nt(parts, placed)
         out_pts[dest] = (tile[16:24] + tile[8:16]) + tile[0:8]
 
+    pl.semaphore_wait(barrier, greeted)
+
+    def points_copy(peer, slot_at):
+        return pltpu.make_async_remote_copy(
+            src_ref=out_pts.at[peer],
+            dst_ref=in_pts.at[slot_at],
+            send_sem=pts_send.at[peer],
+            recv_sem=pts_recv.at[slot_at],
+            device_id=(me_s, peer),
+            device_id_type=MESH,
+        )
+
+    for peer in span_peers:
+        points_copy(peer, me_p).start()
+    in_pts[me_p] = out_pts[me_p]
+
     for load in loads[7:12]:
         load.wait()
     high, low = split2(rows_fwd_f32[...])
@@ -261,22 +277,6 @@
     for matrix, out in ((cols_fwd_f32, cols_fwd), (cols_bwd_f32, cols_bwd)):
         high, low = split2(matrix[...])
         out[...] = jnp.concatenate([high, high, low], axis=0)
-
-    pl.semaphore_wait(barrier, greeted)
-
-    def points_copy(peer, slot_at):
-        return pltpu.make_async_remote_copy(
-            src_ref=out_pts.at[peer],
-            dst_ref=in_pts.at[slot_at],
-            send_sem=pts_send.at[peer],
-            recv_sem=pts_recv.at[slot_at],
-            device_id=(me_s, peer),
-            device_id_type=MESH,
-        )
-
-    for peer in span_peers:
-        points_copy(peer, me_p).start()
-    in_pts[me_p] = out_pts[me_p]
 
     chunks = [slice(c, c + CHUNK) for c in range(0, extent2, CHUNK)]
     for load in loads[12:]:
@@ -533,8 +533,7 @@
             direction = [x + ratio * y for x, y in zip(res, direction + [0.0])]
             norm = norm_next
 
-    for factor, value in zip(factors, pres + res):
-        factor[...] = value[:, 0:1]
+    factors[...] = jnp.concatenate(pres + res + [jnp.zeros((1, LANES), jnp.float32)], axis=0)
 
     for k in range(ITERS + 1):
         store(k).wait()
@@ -550,6 +549,45 @@
             for k in range(ITERS + 1):
                 for q in range(PARTS):
                     halo_copy(k, d, q).wait_send()
+
+
+def outputs_body(pieces, *refs):
+    steps = ITERS + 1
+    basis_in, factors_in, outs = refs[:steps], refs[steps], refs[steps + 1 : steps + 3]
+    factors, basis, made, load_sem, store_sem = refs[steps + 3 :]
+    rows, width = basis.shape[1:]
+    height = rows // pieces
+    first = pltpu.make_async_copy(factors_in, factors, load_sem.at[pieces * steps])
+    first.start()
+
+    def load(n, i):
+        at = pl.ds(n * height, height)
+        return pltpu.make_async_copy(
+            basis_in[i].at[at], basis.at[i, at], load_sem.at[n * steps + i]
+        )
+
+    def store(n, i):
+        at = pl.ds(n * height, height)
+        return pltpu.make_async_copy(made.at[i, at], outs[i].at[at], store_sem.at[n * 2 + i])
+
+    for n in range(pieces):
+        for i in range(steps):
+            load(n, i).start()
+    first.wait()
+    rates = [jnp.broadcast_to(factors[i : i + 1, 0:1], (POLY, width)) for i in range(2 * ITERS + 1)]
+    for n in range(pieces):
+        for i in range(steps):
+            load(n, i).wait()
+        for base in range(n * height, (n + 1) * height, POLY):
+            at = slice(base, base + POLY)
+            vec = [basis[i, at, :] for i in range(steps)]
+            made[0, at, :] = sum(rates[i] * vec[i] for i in range(ITERS))
+            made[1, at, :] = sum(rates[ITERS + i] * vec[i] for i in range(steps))
+        for i in range(2):
+            store(n, i).start()
+    for n in range(pieces):
+        for i in range(2):
+            store(n, i).wait()
 
 
 def on_device(velocity, coefficient, coords, forces, line_id, line_gain, dest_span, owner_element):
@@ -585,9 +623,9 @@
     ]
     outs = pl.pallas_call(
         functools.partial(body, sizes),
-        out_shape=(block,) * steps + (jax.ShapeDtypeStruct((1, 1), f32),) * (2 * ITERS + 1),
+        out_shape=(block,) * steps + (jax.ShapeDtypeStruct((8, LANES), f32),),
         in_specs=[hbm] * N_IN,
-        out_specs=(hbm,) * steps + (vmem,) * (2 * ITERS + 1),
+        out_specs=(hbm,) * steps + (vmem,),
         scratch_shapes=[pltpu.VMEM(x.shape, x.dtype) for x in operands]
         + [
             pltpu.VMEM((2 * rows, 4 * rows), jnp.bfloat16),
@@ -627,12 +665,24 @@
         ),
         name="wind_farm_step",
     )(*operands)
+    pieces = 4
+    pressure, residual = pl.pallas_call(
+        functools.partial(outputs_body, pieces),
+        out_shape=(block, block),
+        in_specs=[hbm] * (steps + 1),
+        out_specs=(hbm, hbm),
+        scratch_shapes=[
+            pltpu.VMEM((8, LANES), f32),
+            pltpu.VMEM((steps, rows, extent2), f32),
+            pltpu.VMEM((2, rows, extent2), f32),
+            pltpu.SemaphoreType.DMA((1 + pieces * steps,)),
+            pltpu.SemaphoreType.DMA((pieces * 2,)),
+        ],
+        compiler_params=pltpu.CompilerParams(vmem_limit_bytes=60 * 1024 * 1024),
+        name="outputs",
+    )(*outs)
     shape = (extent0, extent1, extent2)
-    basis = [vector.reshape(shape) for vector in outs[:steps]]
-    factors = [factor.reshape(()) for factor in outs[steps:]]
-    pressure = sum(factors[i] * basis[i] for i in range(ITERS))
-    residual = sum(factors[ITERS + i] * basis[i] for i in range(steps))
-    return pressure, residual
+    return pressure.reshape(shape), residual.reshape(shape)
 
 
 def solution(mesh):

time: 43.4 us -> 39 us (0.90)
  other arithmetic: 7.1 us -> 0 us
  Pallas kernels: 35.5 us -> 38.2 us
    add x1 -> x0, other arithmetic: 7.1 us -> none  [on_device(): residual = sum((factors[ITERS + i] * basis[i] for i in range(steps)))]
    pallas_call x0 -> x1, Pallas kernels: none -> 2.57 us  [on_device(): pl.pallas_call(functools.partial(outputs_body, pieces), out_shape=(block,...]
where the time goes in v3:
time: 39 us; the launch traced here: 38.8 us
  Pallas kernels  38.2 us (98%)
  between operations  0.64 us (2%)
    pallas_call x1, Pallas kernels, on_device(): pl.pallas_call(functools.partial(body, sizes), out_shape=(block,) * steps...  35.6 us
    pallas_call x1, Pallas kernels, on_device(): pl.pallas_call(functools.partial(outputs_body, pieces), out_shape=(block,...  2.57 us

profile of v3, /device:TPU:0, one launch (start us, length us, event | category | flops | bytes accessed | tf_op | source)
XLA Modules:
  0.0 38.8 jit_solution(16118306415823771234)
XLA Ops:
  0.6 35.6 %wind_farm_step.1 = (f32[128,1024]{1,0:T(8,128)}, f32[128,1024]{1,0:T(8,128)}, f32[128,1024]{1,0:T(8,128)}, f32[128,1024]{1,0:T(8,128)}, f32[8,128]{1,0:T(8,128)}) custom-call(f32[3,128]{1,0:T(4,128)} %refs_0_.1, f32[3,128]{1,0:T(4,128)} %refs_1_.1, s32[1,128]{1,0:T(1,128)} %bitcast.13, f32[1,400]{1,0:T(1,128)} %bitcast.12, s32[1,128]{1,0:T(1,128)} %bitcast.14, ...), custom_call_target="tpu_custom_call" | custom-call | flops 6000000000 | bytes 4194304 | tf_op jit(solution)/shard_map/wind_farm_step/pallas_call | solution.py:624
  36.3 2.6 %outputs.1 = (f32[128,1024]{1,0:T(8,128)}, f32[128,1024]{1,0:T(8,128)}) custom-call(f32[128,1024]{1,0:T(8,128)} %get-tuple-element.9.refs_0_, f32[128,1024]{1,0:T(8,128)} %get-tuple-element.10.refs_1_, f32[128,1024]{1,0:T(8,128)} %get-tuple-element.11.refs_2_, f32[128,1024]{1,0:T(8,128)} %get-tuple-element.12.refs_3_, f32[8,128]{1,0:T(8,128)} %get-tuple-element.13.refs_4_), custom_call_target="tpu_custom_call" | custom-call | tf_op jit(solution)/shard_map/outputs/pallas_call | solution.py:669

commit v4 on v3

--- a/solution.py
+++ b/solution.py
@@ -12,7 +12,7 @@
 ITERS = 3
 LANES = 128
 CHUNK = 256
-PARTS = 4
+PARTS = 2
 N_IN = 14
 
 kernel_width = 0.45
@@ -281,11 +281,28 @@
     chunks = [slice(c, c + CHUNK) for c in range(0, extent2, CHUNK)]
     for load in loads[12:]:
         load.wait()
-    for cols in chunks:
-        w = weight[...]
+    part_width = extent2 // PARTS
+    groups_at = [slice(c.start, c.stop) for c in chunks[: len(chunks) // PARTS]]
+    for start in range(part_width, extent2, part_width):
+        groups_at.append(slice(start, start + part_width))
+
+    def weight_over(cols):
+        return jnp.concatenate([weight[...]] * ((cols.stop - cols.start) // CHUNK), axis=1)
+
+    def times_cols(value, matrix):
+        count = value.shape[1] // CHUNK
+        tall = jnp.concatenate(
+            [value[:, i * CHUNK : (i + 1) * CHUNK] for i in range(count)], axis=0
+        )
+        tall = dot(stacked(tall, 1), matrix[...])
+        return jnp.concatenate([tall[i * rows : (i + 1) * rows] for i in range(count)], axis=1)
+
+    for start in range(0, extent2, part_width):
+        cols = slice(start, start + part_width)
+        w = weight_over(cols)
         both = jnp.concatenate([w * vel[0, :, cols], w * vel[1, :, cols]], axis=0)
-        work[0, :, cols] = dot(rows_bwd[...], stacked(both, 0)) + dot(
-            stacked(w * vel[2, :, cols], 1), cols_bwd[...]
+        work[0, :, cols] = dot(rows_bwd[...], stacked(both, 0)) + times_cols(
+            w * vel[2, :, cols], cols_bwd
         )
         metric[:, cols] = metric[:, cols] * w
 
@@ -330,31 +347,30 @@
     left_pts = stacked(lhs_pts[...], 1)
 
     def tile_sum(value):
-        total = jnp.sum(value.reshape(rows // POLY, POLY, CHUNK), axis=0)
-        return sum(total[:, at : at + LANES] for at in range(0, CHUNK, LANES))
+        total = jnp.sum(value.reshape(rows // POLY, POLY, value.shape[1]), axis=0)
+        return sum(total[:, at : at + LANES] for at in range(0, value.shape[1], LANES))
 
     def rhs_chunk(cols):
         high, low = split2(rhs_pts[cols, :])
         force = dot_nt(left_pts, jnp.concatenate([high, high, low], axis=1))
         work[0, :, cols] = work[0, :, cols] + force
 
-    def operator_chunk(k, cols):
+    def operator_group(k, cols):
         field = basis[k, :, cols]
         high, low = split2(field)
         m = metric[:, cols]
         grad = dot(rows_fwd[...], jnp.concatenate([high, low, high, low], axis=0))
-        grad2 = dot(jnp.concatenate([high, low, high], axis=1), cols_fwd[...])
+        grad2 = times_cols(field, cols_fwd)
         both = jnp.concatenate([grad[:rows] * m, grad[rows:] * m], axis=0)
         out = (
             dot(rows_bwd[...], stacked(both, 0))
-            + dot(stacked(grad2 * m, 1), cols_bwd[...])
-            + weight[...] * field
+            + times_cols(grad2 * m, cols_bwd)
+            + weight_over(cols) * field
         )
         work[k + 1, :, cols] = out
         return tile_sum(field * work[k, :, cols]), tile_sum(field * out)
 
     last0, last1 = extent0 - 1, extent1 - 1
-    part_width = extent2 // PARTS
 
     def halo_copy(k, d, q):
         cols = pl.ds(q * part_width, part_width)
@@ -443,35 +459,34 @@
                 x[:, inner] + jnp.where(first2, lower, 0.0) + jnp.where(last2, upper, 0.0)
             )
 
-    per_part = len(chunks) // PARTS
-
     def store(k):
         return pltpu.make_async_copy(basis.at[k], basis_out[k], store_sem.at[k])
 
-    def joined_chunks(k):
+    def joined_groups(k):
         have = 0
-        for n, cols in enumerate(chunks):
-            need = min((n + 1) // per_part + 1, PARTS)
+        for cols in groups_at:
+            need = min(cols.stop // part_width + 1, PARTS)
             while have < need:
                 join(k, have)
                 have += 1
-            assemble(k, cols)
-            if n + 1 == len(chunks):
+            for start in range(cols.start, cols.stop, CHUNK):
+                assemble(k, slice(start, start + CHUNK))
+            if cols.stop == extent2:
                 store(k).start()
-            yield n, cols
-
-    for n, cols in enumerate(chunks):
+            yield cols
+
+    for cols in chunks:
         rhs_chunk(cols)
-        if (n + 1) % per_part == 0:
-            send_faces(0, n // per_part)
+        if cols.stop % part_width == 0:
+            send_faces(0, cols.stop // part_width - 1)
     mine = []
     for k in range(ITERS):
         even = odd = 0.0
-        for n, cols in joined_chunks(k):
-            more = operator_chunk(k, cols)
+        for cols in joined_groups(k):
+            more = operator_group(k, cols)
             even, odd = even + more[0], odd + more[1]
-            if (n + 1) % per_part == 0:
-                send_faces(k + 1, n // per_part)
+            if cols.stop % part_width == 0:
+                send_faces(k + 1, cols.stop // part_width - 1)
         mine += [even, odd]
 
     mine = [jnp.sum(total, axis=0, keepdims=True) for total in mine]
@@ -508,7 +523,7 @@
     sums2[me_s] = total
     for peer in stream_peers:
         sum2_copy(peer, me_s).start()
-    for _ in joined_chunks(ITERS):
+    for _ in joined_groups(ITERS):
         pass
     for peer in stream_peers:
         sum2_copy(peer, peer).wait_recv()

time: 39 us -> 39 us (level)
  no operation moved by 1% of the time
where the time goes in v4:
time: 39 us; the launch traced here: 38.8 us
  Pallas kernels  38.2 us (98%)
  between operations  0.64 us (2%)
    pallas_call x1, Pallas kernels, on_device(): pl.pallas_call(functools.partial(body, sizes), out_shape=(block,) * steps...  35.6 us
    pallas_call x1, Pallas kernels, on_device(): pl.pallas_call(functools.partial(outputs_body, pieces), out_shape=(block,...  2.57 us

profile of v4, /device:TPU:0, one launch (start us, length us, event | category | flops | bytes accessed | tf_op | source)
XLA Modules:
  0.0 38.8 jit_solution(9189328008387284085)
XLA Ops:
  0.6 35.6 %wind_farm_step.1 = (f32[128,1024]{1,0:T(8,128)}, f32[128,1024]{1,0:T(8,128)}, f32[128,1024]{1,0:T(8,128)}, f32[128,1024]{1,0:T(8,128)}, f32[8,128]{1,0:T(8,128)}) custom-call(f32[3,128]{1,0:T(4,128)} %refs_0_.1, f32[3,128]{1,0:T(4,128)} %refs_1_.1, s32[1,128]{1,0:T(1,128)} %bitcast.13, f32[1,400]{1,0:T(1,128)} %bitcast.12, s32[1,128]{1,0:T(1,128)} %bitcast.14, ...), custom_call_target="tpu_custom_call" | custom-call | flops 6000000000 | bytes 4194304 | tf_op jit(solution)/shard_map/wind_farm_step/pallas_call | solution.py:639
  36.3 2.6 %outputs.1 = (f32[128,1024]{1,0:T(8,128)}, f32[128,1024]{1,0:T(8,128)}) custom-call(f32[128,1024]{1,0:T(8,128)} %get-tuple-element.9.refs_0_, f32[128,1024]{1,0:T(8,128)} %get-tuple-element.10.refs_1_, f32[128,1024]{1,0:T(8,128)} %get-tuple-element.11.refs_2_, f32[128,1024]{1,0:T(8,128)} %get-tuple-element.12.refs_3_, f32[8,128]{1,0:T(8,128)} %get-tuple-element.13.refs_4_), custom_call_target="tpu_custom_call" | custom-call | tf_op jit(solution)/shard_map/outputs/pallas_call | solution.py:684

commit v5 on v4

--- a/solution.py
+++ b/solution.py
@@ -391,6 +391,13 @@
         )
 
     def send_faces(k, q):
+        def start(d):
+            @pl.when(exists(OFFSETS[d]))
+            def _():
+                halo_copy(k, d, q).start()
+
+        start(0)
+        start(1)
         cols = slice(q * part_width, (q + 1) * part_width)
         for a in range(extent0):
             top = work[k, a * extent1 + last1 : a * extent1 + last1 + 1, cols]
@@ -403,11 +410,8 @@
             if a == 0:
                 send_edge[k, 2, :, cols] = top
                 send_edge[k, 3, :, cols] = bottom
-        for d in range(8):
-
-            @pl.when(exists(OFFSETS[d]))
-            def _(d=d):
-                halo_copy(k, d, q).start()
+        for d in range(2, 8):
+            start(d)
 
     def join(k, q):
         for d in (2, 3, 4, 5, 6, 7, 0, 1):

time: 39 us -> 39 us (level)
  no operation moved by 1% of the time
where the time goes in v5:
time: 39 us; the launch traced here: 38.8 us
  Pallas kernels  38.1 us (98%)
  between operations  0.64 us (2%)
    pallas_call x1, Pallas kernels, on_device(): pl.pallas_call(functools.partial(body, sizes), out_shape=(block,) * steps...  35.6 us
    pallas_call x1, Pallas kernels, on_device(): pl.pallas_call(functools.partial(outputs_body, pieces), out_shape=(block,...  2.57 us

profile of v5, /device:TPU:0, one launch (start us, length us, event | category | flops | bytes accessed | tf_op | source)
XLA Modules:
  0.0 38.8 jit_solution(4335028311285980132)
XLA Ops:
  0.6 35.6 %wind_farm_step.1 = (f32[128,1024]{1,0:T(8,128)}, f32[128,1024]{1,0:T(8,128)}, f32[128,1024]{1,0:T(8,128)}, f32[128,1024]{1,0:T(8,128)}, f32[8,128]{1,0:T(8,128)}) custom-call(f32[3,128]{1,0:T(4,128)} %refs_0_.1, f32[3,128]{1,0:T(4,128)} %refs_1_.1, s32[1,128]{1,0:T(1,128)} %bitcast.13, f32[1,400]{1,0:T(1,128)} %bitcast.12, s32[1,128]{1,0:T(1,128)} %bitcast.14, ...), custom_call_target="tpu_custom_call" | custom-call | flops 6000000000 | bytes 4194304 | tf_op jit(solution)/shard_map/wind_farm_step/pallas_call | solution.py:643
  36.2 2.6 %outputs.1 = (f32[128,1024]{1,0:T(8,128)}, f32[128,1024]{1,0:T(8,128)}) custom-call(f32[128,1024]{1,0:T(8,128)} %get-tuple-element.9.refs_0_, f32[128,1024]{1,0:T(8,128)} %get-tuple-element.10.refs_1_, f32[128,1024]{1,0:T(8,128)} %get-tuple-element.11.refs_2_, f32[128,1024]{1,0:T(8,128)} %get-tuple-element.12.refs_3_, f32[8,128]{1,0:T(8,128)} %get-tuple-element.13.refs_4_), custom_call_target="tpu_custom_call" | custom-call | tf_op jit(solution)/shard_map/outputs/pallas_call | solution.py:688
